TPU v7x, 128 devices: a whole 4x4x4 slice. The times are simulated.
128 devices in a mesh: sec: 8 (over x, core), op: 16 (over y, z).
Axes of the slice: x: 4, y: 4, z: 4, core: 2. Of those that a mesh axis runs over, the one named last changes fastest.
Arguments:
- psi: bfloat16 [8192, 256], P(('sec', 'op')), may hold values from -6 to 6
- left_env: bfloat16 [384, 32, 256, 256], P('op', 'sec'), may hold values from -0.01953125 to 0.01953125
- right_env: bfloat16 [384, 32, 256, 256], P('op', 'sec'), may hold values from -0.375 to 0.375
- term_src: int32 [384, 32], P('op', 'sec'), may hold values from 0 to 31, as said below
- block_dims: int32 [2, 32], replicated, may hold values from 64 to 256, as said below
Outputs:
- sigma: bfloat16 [8192, 256], P(('sec', 'op'))
Inputs may be any that keep to these rules, and one draw needn't show every extreme that they name: |term_src[t, k] - k| <= 2 for every t and k, and term_src[t, k] = k + 2 for some t and k. `block_dims`: every entry is a multiple of 4; 256 is reached in each row.
All inputs are finite; a program needn't handle non-finite values.
Results may differ from a plain program's by a relative error of at most 0.0049.
Values may be sent and summed in bfloat16 or wider, within the bound.
A program may use at most 128 MiB of HBM per device.

v0:
```python
import jax
import jax.numpy as jnp
from jax import lax
from jax.sharding import PartitionSpec as P


def padded(cells, sides, width):
    for axis, dim in sides:
        count = lax.axis_size(axis)
        ends = count - 1
        head = lax.slice_in_dim(cells, 0, width, axis=dim)
        tail = lax.slice_in_dim(cells, cells.shape[dim] - width, cells.shape[dim], axis=dim)
        cells = jnp.concatenate(
            [
                lax.ppermute(tail, axis, [(i, (i + 1) % count) for i in range(ends)]),
                cells,
                lax.ppermute(head, axis, [((i + 1) % count, i) for i in range(ends)]),
            ],
            axis=dim,
        )
    return cells


def lookup_dims(block_ids, block_dims):
    count = block_dims.shape[1]
    every_id = jnp.arange(count, dtype=jnp.int32)
    match = block_ids[..., None] == every_id
    rows_used = jnp.sum(jnp.where(match, block_dims[0], 0), axis=-1)
    cols_used = jnp.sum(jnp.where(match, block_dims[1], 0), axis=-1)
    return (rows_used, cols_used)


def shards(psi, left_env, right_env, term_src, block_dims):
    side = psi.shape[1]
    per_sec = left_env.shape[1]
    local_rows = psi.shape[0]
    group_size = lax.axis_size("op")
    extended = padded(psi, (("sec", 0),), local_rows)
    gathered = lax.all_gather(extended, "op", axis=0, tiled=True)
    arranged = gathered.reshape(group_size, 3, local_rows, side).transpose(1, 0, 2, 3)
    blocks = arranged.reshape(-1, side, side)
    first_block = lax.axis_index("sec") * per_sec - per_sec
    local_src = term_src - first_block
    selected = jnp.take(blocks, local_src, axis=0)
    places = jnp.arange(side, dtype=jnp.int32)
    rows_used, cols_used = lookup_dims(term_src, block_dims)
    keep = (places[:, None] < rows_used[..., None, None]) & (
        places[None, :] < cols_used[..., None, None]
    )
    masked = jnp.where(keep, selected, jnp.zeros_like(selected))
    half = jnp.einsum(
        "tkij,tkjl->tkil", masked, right_env, preferred_element_type=jnp.float32
    ).astype(jnp.bfloat16)
    partial_value = jnp.einsum("tkij,tkjl->kil", left_env, half, preferred_element_type=jnp.float32)
    partial_value = partial_value.reshape(per_sec * side, side)
    summed = lax.psum_scatter(partial_value, "op", scatter_dimension=0, tiled=True)
    row_start = (lax.axis_index("sec") * group_size + lax.axis_index("op")) * local_rows
    global_rows = row_start + jnp.arange(local_rows, dtype=jnp.int32)
    out_blocks = global_rows // side
    inner_rows = global_rows % side
    out_rows_used, out_cols_used = lookup_dims(out_blocks, block_dims)
    out_keep = (inner_rows < out_rows_used)[:, None] & (places[None, :] < out_cols_used[:, None])
    return jnp.where(out_keep, summed, jnp.zeros_like(summed)).astype(jnp.bfloat16)


def solution(mesh):
    placed = (
        P(("sec", "op"), None),
        P("op", "sec", None, None),
        P("op", "sec", None, None),
        P("op", "sec"),
        P(),
    )
    return jax.shard_map(
        shards, mesh=mesh, in_specs=placed, out_specs=P(("sec", "op"), None), check_vma=False
    )
```

profile of v0, /device:TPU:0, one launch (start us, length us, event | category | flops | bytes accessed | tf_op | source)
XLA Modules:
  0.0 178.6 jit_solution(1798577908962675282)
XLA Ops:
  6.5 0.0 all-gather.2.cloned.1.call-start
  6.5 1.3 collective-permute-start
  7.8 1.3 collective-permute-start.1
  9.1 0.0 collective-permute-done
  9.1 3.8 %collective-permute-done.1 = bf16[64,256]{1,0:T(8,128)(2,1)S(1)} collective-permute-done((bf16[64,256]{1,0:T(8,128)(2,1)}, bf16[64,256]{1,0:T(8,128)(2,1)S(1)}, u32[]{:S(2)}, u32[]{:S(2)}) %collective-permute-start.1) | collective-permute-done | bytes 32800 | tf_op jit(solution)/shard_map/ppermute | solution.py:17
  12.9 1.4 pad_maximum_fusion
  14.3 0.0 all-gather.2.cloned.1.call-update
  14.4 0.0 reduce-scatter.2.cloned.1.call-start
  14.4 0.7 compare_and_fusion
  15.1 0.1 copy.21
  15.2 0.1 reshape.72
  15.3 0.8 slice_bitcast_fusion
  16.1 1.0 select_reduce_fusion.1
  17.0 0.1 iota_compare_fusion
  17.1 45.8 %all-gather.2.cloned.1.call-done = bf16[3072,256]{1,0:T(8,128)(2,1)} async-done(((bf16[192,256]{1,0:T(8,128)(2,1)}), bf16[3072,256]{1,0:T(8,128)(2,1)}) %all-gather.2.cloned.1.call-update) | async-done | bytes 1572880 | tf_op jit(solution)/shard_map/all_gather | solution.py:39
  63.0 1.5 copy.20
  64.5 6.7 %gather_fusion = bf16[96,256,256]{2,1,0:T(8,128)(2,1)} fusion(bf16[12,256,256]{2,1,0:T(8,128)(2,1)S(1)} %bitcast.16, s32[1024]{0:T(1024)S(1)} %pad_clamp_fusion), kind=kCustom, calls=%fused_computation | custom fusion | bytes 25166208 | tf_op jit(solution)/shard_map/jit(_take)/gather | solution.py:44
  71.2 13.9 %fusion.26 = bf16[24,4,256,256]{3,2,0,1:T(8,128)(2,1)} fusion(bf16[24,4,256,256]{3,2,1,0:T(8,128)(2,1)} %param.7, bf16[24,4,256,256]{3,2,1,0:T(8,128)(2,1)} %bitcast.17, pred[24,4]{0,1:T(4,128)(4,1)S(1)} %get-tuple-element.9, pred[24,4,256]{2,0,1:T(8,128)(4,1)S(1)} %get-tuple-element.13, pred[24,4,256]{2,0,1:T(8,128)(4,1)S(1)} %get-tuple-element.14), kind=kOutput, calls=%fused_computation.7.clone.1 | convolution fusion | flops 3246391296 | bytes 37797984 | tf_op jit(solution)/shard_map/tkij,tkjl->tkil/dot_general | solution.py:51
  85.1 12.6 %fusion.1 = f32[4,256,256,1]{1,2,3,0:T(8,128)} fusion(bf16[24,4,256,256]{3,2,1,0:T(8,128)(2,1)} %param.6, bf16[24,4,256,256]{3,2,0,1:T(8,128)(2,1)} %fusion.26), kind=kOutput, calls=%fused_computation.3 | convolution fusion | flops 3221225472 | bytes 26214400 | tf_op jit(solution)/shard_map/tkij,tkjl->kil/dot_general | solution.py:54
  97.7 0.0 reduce-scatter.2.cloned.1.call-update
  97.8 0.1 select_reduce_fusion.3
  97.9 72.4 %reduce-scatter.2.cloned.1.call-done = f32[64,256]{1,0:T(8,128)} async-done(((f32[1024,256]{1,0:T(8,128)}), f32[64,256]{1,0:T(8,128)}) %reduce-scatter.2.cloned.1.call-update) | async-done | bytes 65552 | tf_op jit(solution)/shard_map/reduce_scatter | solution.py:56
  170.2 1.5 select_convert_fusion
  (3 shorter events, 0.0 us)
Async XLA Ops:
  6.5 56.4 %all-gather.2.cloned.1.call-start = ((), (), s32[]{:S(2)}) async-start(), calls=%async_computation.1 | async-start | bytes 1671168 | tf_op jit(solution)/shard_map/all_gather | solution.py:39
  6.5 2.6 %collective-permute-start = (bf16[64,256]{1,0:T(8,128)(2,1)}, bf16[64,256]{1,0:T(8,128)(2,1)S(1)}, u32[]{:S(2)}, u32[]{:S(2)}) collective-permute-start(bf16[64,256]{1,0:T(8,128)(2,1)} %param.5), channel_id=1, source_target_pairs={{0,16},{16,32},{32,48},{48,64},{64,80},{80,96},{96,112},{1,17},{17... | collective-permute-start | bytes 98312 | tf_op jit(solution)/shard_map/ppermute | solution.py:15
  7.8 5.1 %collective-permute-start.1 = (bf16[64,256]{1,0:T(8,128)(2,1)}, bf16[64,256]{1,0:T(8,128)(2,1)S(1)}, u32[]{:S(2)}, u32[]{:S(2)}) collective-permute-start(bf16[64,256]{1,0:T(8,128)(2,1)} %param.5), channel_id=1, source_target_pairs={{16,0},{32,16},{48,32},{64,48},{80,64},{96,80},{112,96},{17,1},{33... | collective-permute-start | bytes 98312 | tf_op jit(solution)/shard_map/ppermute | solution.py:17
  14.4 155.9 %reduce-scatter.2.cloned.1.call-start = ((), (), s32[]{:S(2)}) async-start(), calls=%async_computation.2 | async-start | bytes 1114112 | tf_op jit(solution)/shard_map/reduce_scatter | solution.py:56
Sparse Core Ops, SparseCore 0:
  14.5 48.4 all-gather.1
  97.8 72.3 reduce-scatter.1
where the time goes:
time: 179 us
  waiting for transfers between devices  122 us (68%)
  matrix products  26.5 us (15%)
  between operations  13.5 us (8%)
  local copies, waits for them, and re-layouts  9.16 us (5%)
  other arithmetic  4.82 us (3%)
  starting transfers between devices  2.62 us (1%)
    reduce_scatter x1, waiting for transfers between devices, shards(): lax.psum_scatter(partial_value, 'op', scatter_dimension=0, tiled=True)  72.4 us
    all_gather x1, waiting for transfers between devices, shards(): gathered = lax.all_gather(extended, 'op', axis=0, tiled=True)  45.8 us
    dot_general x1, matrix products, shards(): jnp.einsum('tkij,tkjl->tkil', masked, right_env, preferred_element_type=j...  13.9 us
    dot_general x1, matrix products, shards(): jnp.einsum('tkij,tkjl->kil', left_env, half, preferred_element_type=jnp.f...  12.6 us
    gather x1, local copies, waits for them, and re-layouts, shards(): selected = jnp.take(blocks, local_src, axis=0)  6.71 us
    ppermute x1, waiting for transfers between devices, padded(): lax.ppermute(head, axis, [((i + 1) % count, i) for i in range(ends)])  3.81 us
  transfers between devices with their start and end apart: 4, of which 3 were waited for; matrix products, arithmetic and copies ran while one was open for 2% of the time, Pallas kernels for 0%

commit v1 on v0

--- a/solution.py
+++ b/solution.py
@@ -31,12 +31,33 @@
 
 
 def shards(psi, left_env, right_env, term_src, block_dims):
+
+    def perform_thing_for(vals):
+        seen_now, built, near = (lax.axis_size("op"), lax.axis_index("op"), vals.shape[0])
+        crops = [(no, (no + 1) % seen_now) for no in range(seen_now)]
+        passed = jnp.zeros((*vals.shape[:0], seen_now * near, *vals.shape[1:]), vals.dtype)
+        passed = lax.dynamic_update_slice_in_dim(passed, vals, built * near, axis=0)
+        right_arr = earlier = vals
+        u1 = seen_now // 2
+        rack = [(no, (no - 1) % seen_now) for no in range(seen_now)]
+        for idx in range(1, u1 + 1):
+            right_arr = lax.ppermute(right_arr, "op", crops)
+            passed = lax.dynamic_update_slice_in_dim(
+                passed, right_arr, (built - idx) % seen_now * near, axis=0
+            )
+            if idx < seen_now - u1:
+                earlier = lax.ppermute(earlier, "op", rack)
+                passed = lax.dynamic_update_slice_in_dim(
+                    passed, earlier, (built + idx) % seen_now * near, axis=0
+                )
+        return passed
+
     side = psi.shape[1]
     per_sec = left_env.shape[1]
     local_rows = psi.shape[0]
     group_size = lax.axis_size("op")
     extended = padded(psi, (("sec", 0),), local_rows)
-    gathered = lax.all_gather(extended, "op", axis=0, tiled=True)
+    gathered = perform_thing_for(extended)
     arranged = gathered.reshape(group_size, 3, local_rows, side).transpose(1, 0, 2, 3)
     blocks = arranged.reshape(-1, side, side)
     first_block = lax.axis_index("sec") * per_sec - per_sec

time: 179 us -> 199 us (1.11)
  starting transfers between devices: 2.62 us -> 44.2 us
  waiting for transfers between devices: 122 us -> 101 us
    all_gather x1 -> x0, waiting for transfers between devices: 45.8 us -> none  [shards(): gathered = lax.all_gather(extended, 'op', axis=0, tiled=True)]
    ppermute x0 -> x15, starting transfers between devices: none -> 41.6 us  [the longest x7 41.6 us: perform_thing_for(): earlier = lax.ppermute(earlier, 'op', rack)]
    ppermute x0 -> x15, waiting for transfers between devices: none -> 29.8 us  [the longest x8 17.2 us: perform_thing_for(): right_arr = lax.ppermute(right_arr, 'op', crops)]
    ppermute x1, waiting for transfers between devices: 3.81 us -> 0.01 us  [padded(): lax.ppermute(head, axis, [((i + 1) % count, i) for i in range(ends)])]
  transfers between devices with their start and end apart: 4 -> 18, of which waited for: 3 -> 14; matrix products, arithmetic and copies ran while one was open for 2% -> 2% of each run, Pallas kernels for 0% -> 0%
where the time goes in v1:
time: 199 us; the launch traced here: 198 us
  waiting for transfers between devices  101 us (51%)
  starting transfers between devices  44.2 us (22%)
  matrix products  26.5 us (13%)
  between operations  13.9 us (7%)
  local copies, waits for them, and re-layouts  8.89 us (4%)
  other arithmetic  3.43 us (2%)
    reduce_scatter x1, waiting for transfers between devices, shards(): lax.psum_scatter(partial_value, 'op', scatter_dimension=0, tiled=True)  71.6 us
    ppermute x7, starting transfers between devices, perform_thing_for(): earlier = lax.ppermute(earlier, 'op', rack)  41.6 us
    ppermute x8, waiting for transfers between devices, perform_thing_for(): right_arr = lax.ppermute(right_arr, 'op', crops)  17.2 us
    dot_general x1, matrix products, shards(): jnp.einsum('tkij,tkjl->tkil', masked, right_env, preferred_element_type=j...  13.9 us
    ppermute x7, waiting for transfers between devices, perform_thing_for(): earlier = lax.ppermute(earlier, 'op', rack)  12.6 us
    dot_general x1, matrix products, shards(): jnp.einsum('tkij,tkjl->kil', left_env, half, preferred_element_type=jnp.f...  12.6 us
    gather x1, local copies, waits for them, and re-layouts, shards(): selected = jnp.take(blocks, local_src, axis=0)  6.72 us
  transfers between devices with their start and end apart: 18, of which 14 were waited for; matrix products, arithmetic and copies ran while one was open for 2% of the time, Pallas kernels for 0%

profile of v1, /device:TPU:0, one launch (start us, length us, event | category | flops | bytes accessed | tf_op | source)
XLA Modules:
  0.0 198.4 jit_solution(15223587420924496442)
XLA Ops:
  6.5 1.3 collective-permute-start
  7.8 1.3 collective-permute-start.1
  9.1 0.8 slice_bitcast_fusion
  9.9 0.7 compare_and_fusion
  10.8 1.0 select_reduce_fusion.1
  12.2 0.8 constant_dynamic-update-slice_fusion.1
  13.0 7.1 %collective-permute-start.3 = (bf16[192,256]{1,0:T(8,128)(2,1)S(1)}, bf16[192,256]{1,0:T(8,128)(2,1)S(1)}, u32[]{:S(2)}, u32[]{:S(2)}) collective-permute-start(bf16[192,256]{1,0:T(8,128)(2,1)S(1)} %constant_dynamic-update-slice_fusion), channel_id=1, source_target_pairs={{0,15},{1,0},{2,1},{3,2},{4,3},{5,4},{6,5},{7,6},{8,7},{9,8},{10,9... | collective-permute-start | bytes 294920 | tf_op jit(solution)/shard_map/ppermute | solution.py:49
  20.2 2.1 %collective-permute-done.3 = bf16[192,256]{1,0:T(8,128)(2,1)S(1)} collective-permute-done((bf16[192,256]{1,0:T(8,128)(2,1)S(1)}, bf16[192,256]{1,0:T(8,128)(2,1)S(1)}, u32[]{:S(2)}, u32[]{:S(2)}) %collective-permute-start.3) | collective-permute-done | bytes 98336 | tf_op jit(solution)/shard_map/ppermute | solution.py:49
  22.3 5.7 %collective-permute-start.5 = (bf16[192,256]{1,0:T(8,128)(2,1)S(1)}, bf16[192,256]{1,0:T(8,128)(2,1)S(1)}, u32[]{:S(2)}, u32[]{:S(2)}) collective-permute-start(bf16[192,256]{1,0:T(8,128)(2,1)S(1)} %collective-permute-done.3), channel_id=1, source_target_pairs={{0,15},{1,0},{2,1},{3,2},{4,3},{5,4},{6,5},{7,6},{8,7},{9,8},{10,9... | collective-permute-start | bytes 294920 | tf_op jit(solution)/shard_map/ppermute | solution.py:49
  28.0 2.9 %collective-permute-done.5 = bf16[192,256]{1,0:T(8,128)(2,1)S(1)} collective-permute-done((bf16[192,256]{1,0:T(8,128)(2,1)S(1)}, bf16[192,256]{1,0:T(8,128)(2,1)S(1)}, u32[]{:S(2)}, u32[]{:S(2)}) %collective-permute-start.5) | collective-permute-done | bytes 98336 | tf_op jit(solution)/shard_map/ppermute | solution.py:49
  30.9 5.8 %collective-permute-start.7 = (bf16[192,256]{1,0:T(8,128)(2,1)S(1)}, bf16[192,256]{1,0:T(8,128)(2,1)S(1)}, u32[]{:S(2)}, u32[]{:S(2)}) collective-permute-start(bf16[192,256]{1,0:T(8,128)(2,1)S(1)} %collective-permute-done.5), channel_id=1, source_target_pairs={{0,15},{1,0},{2,1},{3,2},{4,3},{5,4},{6,5},{7,6},{8,7},{9,8},{10,9... | collective-permute-start | bytes 294920 | tf_op jit(solution)/shard_map/ppermute | solution.py:49
  36.7 0.3 collective-permute-done.4
  37.0 2.0 %collective-permute-done.7 = bf16[192,256]{1,0:T(8,128)(2,1)S(1)} collective-permute-done((bf16[192,256]{1,0:T(8,128)(2,1)S(1)}, bf16[192,256]{1,0:T(8,128)(2,1)S(1)}, u32[]{:S(2)}, u32[]{:S(2)}) %collective-permute-start.7) | collective-permute-done | bytes 98336 | tf_op jit(solution)/shard_map/ppermute | solution.py:49
  39.0 5.8 %collective-permute-start.9 = (bf16[192,256]{1,0:T(8,128)(2,1)S(1)}, bf16[192,256]{1,0:T(8,128)(2,1)S(1)}, u32[]{:S(2)}, u32[]{:S(2)}) collective-permute-start(bf16[192,256]{1,0:T(8,128)(2,1)S(1)} %collective-permute-done.7), channel_id=1, source_target_pairs={{0,15},{1,0},{2,1},{3,2},{4,3},{5,4},{6,5},{7,6},{8,7},{9,8},{10,9... | collective-permute-start | bytes 294920 | tf_op jit(solution)/shard_map/ppermute | solution.py:49
  44.8 0.3 collective-permute-done.6
  45.1 1.9 collective-permute-done.9
  47.0 5.7 %collective-permute-start.11 = (bf16[192,256]{1,0:T(8,128)(2,1)S(1)}, bf16[192,256]{1,0:T(8,128)(2,1)S(1)}, u32[]{:S(2)}, u32[]{:S(2)}) collective-permute-start(bf16[192,256]{1,0:T(8,128)(2,1)S(1)} %collective-permute-done.9), channel_id=1, source_target_pairs={{0,15},{1,0},{2,1},{3,2},{4,3},{5,4},{6,5},{7,6},{8,7},{9,8},{10,9... | collective-permute-start | bytes 294920 | tf_op jit(solution)/shard_map/ppermute | solution.py:49
  52.8 0.3 collective-permute-done.8
  53.1 1.9 collective-permute-done.11
  55.0 5.7 %collective-permute-start.13 = (bf16[192,256]{1,0:T(8,128)(2,1)S(1)}, bf16[192,256]{1,0:T(8,128)(2,1)S(1)}, u32[]{:S(2)}, u32[]{:S(2)}) collective-permute-start(bf16[192,256]{1,0:T(8,128)(2,1)S(1)} %collective-permute-done.11), channel_id=1, source_target_pairs={{0,15},{1,0},{2,1},{3,2},{4,3},{5,4},{6,5},{7,6},{8,7},{9,8},{10,9... | collective-permute-start | bytes 294920 | tf_op jit(solution)/shard_map/ppermute | solution.py:49
  60.7 0.3 collective-permute-done.10
  61.0 1.9 collective-permute-done.13
  62.9 5.7 %collective-permute-start.15 = (bf16[192,256]{1,0:T(8,128)(2,1)S(1)}, bf16[192,256]{1,0:T(8,128)(2,1)S(1)}, u32[]{:S(2)}, u32[]{:S(2)}) collective-permute-start(bf16[192,256]{1,0:T(8,128)(2,1)S(1)} %collective-permute-done.13), channel_id=1, source_target_pairs={{0,15},{1,0},{2,1},{3,2},{4,3},{5,4},{6,5},{7,6},{8,7},{9,8},{10,9... | collective-permute-start | bytes 294920 | tf_op jit(solution)/shard_map/ppermute | solution.py:49
  68.6 0.3 collective-permute-done.12
  69.0 7.9 %collective-permute-done.14 = bf16[192,256]{1,0:T(8,128)(2,1)S(1)} collective-permute-done((bf16[192,256]{1,0:T(8,128)(2,1)S(1)}, bf16[192,256]{1,0:T(8,128)(2,1)S(1)}, u32[]{:S(2)}, u32[]{:S(2)}) %collective-permute-start.14) | collective-permute-done | bytes 98336 | tf_op jit(solution)/shard_map/ppermute | solution.py:44
  76.9 7.9 %collective-permute-done.16 = bf16[192,256]{1,0:T(8,128)(2,1)S(1)} collective-permute-done((bf16[192,256]{1,0:T(8,128)(2,1)S(1)}, bf16[192,256]{1,0:T(8,128)(2,1)S(1)}, u32[]{:S(2)}, u32[]{:S(2)}) %collective-permute-start.16) | collective-permute-done | bytes 98336 | tf_op jit(solution)/shard_map/ppermute | solution.py:44
  84.8 0.2 copy.20
  85.0 6.7 %gather_fusion = bf16[96,256,256]{2,1,0:T(8,128)(2,1)} fusion(bf16[12,256,256]{2,1,0:T(8,128)(2,1)S(1)} %bitcast.16, s32[1024]{0:T(1024)S(1)} %pad_clamp_fusion), kind=kCustom, calls=%fused_computation | custom fusion | bytes 25166208 | tf_op jit(solution)/shard_map/jit(_take)/gather | solution.py:65
  91.7 13.9 %fusion.26 = bf16[24,4,256,256]{3,2,0,1:T(8,128)(2,1)} fusion(bf16[24,4,256,256]{3,2,1,0:T(8,128)(2,1)} %param.7, bf16[24,4,256,256]{3,2,1,0:T(8,128)(2,1)} %bitcast.17, pred[24,4]{0,1:T(4,128)(4,1)S(1)} %get-tuple-element.9, pred[24,4,256]{2,0,1:T(8,128)(4,1)S(1)} %get-tuple-element.13, pred[24,4,256]{2,0,1:T(8,128)(4,1)S(1)} %get-tuple-element.14), kind=kOutput, calls=%fused_computation.7.clone.1 | convolution fusion | flops 3246391296 | bytes 37797984 | tf_op jit(solution)/shard_map/tkij,tkjl->tkil/dot_general | solution.py:72
  105.6 12.6 %fusion.1 = f32[4,256,256,1]{1,2,3,0:T(8,128)} fusion(bf16[24,4,256,256]{3,2,1,0:T(8,128)(2,1)} %param.6, bf16[24,4,256,256]{3,2,0,1:T(8,128)(2,1)} %fusion.26), kind=kOutput, calls=%fused_computation.3 | convolution fusion | flops 3221225472 | bytes 26214400 | tf_op jit(solution)/shard_map/tkij,tkjl->kil/dot_general | solution.py:75
  118.4 71.6 %reduce-scatter.2.cloned.1.call-done = f32[64,256]{1,0:T(8,128)} async-done(((f32[1024,256]{1,0:T(8,128)}), f32[64,256]{1,0:T(8,128)}) %reduce-scatter.2.cloned.1.call-update) | async-done | bytes 65552 | tf_op jit(solution)/shard_map/reduce_scatter | solution.py:77
  190.0 1.5 select_convert_fusion
  (40 shorter events, 0.8 us)
Async XLA Ops:
  6.5 183.4 %reduce-scatter.2.cloned.1.call-start = ((), (), s32[]{:S(2)}) async-start(), calls=%async_computation.1 | async-start | bytes 1114112 | tf_op jit(solution)/shard_map/reduce_scatter | solution.py:77
  6.5 5.6 %collective-permute-start = (bf16[64,256]{1,0:T(8,128)(2,1)}, bf16[64,256]{1,0:T(8,128)(2,1)S(1)}, u32[]{:S(2)}, u32[]{:S(2)}) collective-permute-start(bf16[64,256]{1,0:T(8,128)(2,1)} %param.5), channel_id=1, source_target_pairs={{0,16},{16,32},{32,48},{48,64},{64,80},{80,96},{96,112},{1,17},{17... | collective-permute-start | bytes 98312 | tf_op jit(solution)/shard_map/ppermute | solution.py:15
  7.8 5.1 %collective-permute-start.1 = (bf16[64,256]{1,0:T(8,128)(2,1)}, bf16[64,256]{1,0:T(8,128)(2,1)S(1)}, u32[]{:S(2)}, u32[]{:S(2)}) collective-permute-start(bf16[64,256]{1,0:T(8,128)(2,1)} %param.5), channel_id=1, source_target_pairs={{16,0},{32,16},{48,32},{64,48},{80,64},{96,80},{112,96},{17,1},{33... | collective-permute-start | bytes 98312 | tf_op jit(solution)/shard_map/ppermute | solution.py:17
  13.0 9.3 %collective-permute-start.3 = (bf16[192,256]{1,0:T(8,128)(2,1)S(1)}, bf16[192,256]{1,0:T(8,128)(2,1)S(1)}, u32[]{:S(2)}, u32[]{:S(2)}) collective-permute-start(bf16[192,256]{1,0:T(8,128)(2,1)S(1)} %constant_dynamic-update-slice_fusion), channel_id=1, source_target_pairs={{0,15},{1,0},{2,1},{3,2},{4,3},{5,4},{6,5},{7,6},{8,7},{9,8},{10,9... | collective-permute-start | bytes 294920 | tf_op jit(solution)/shard_map/ppermute | solution.py:49
  20.0 7.9 %collective-permute-start.2 = (bf16[192,256]{1,0:T(8,128)(2,1)S(1)}, bf16[192,256]{1,0:T(8,128)(2,1)S(1)}, u32[]{:S(2)}, u32[]{:S(2)}) collective-permute-start(bf16[192,256]{1,0:T(8,128)(2,1)S(1)} %constant_dynamic-update-slice_fusion), channel_id=1, source_target_pairs={{0,1},{1,2},{2,3},{3,4},{4,5},{5,6},{6,7},{7,8},{8,9},{9,10},{10,1... | collective-permute-start | bytes 294920 | tf_op jit(solution)/shard_map/ppermute | solution.py:44
  22.3 8.6 %collective-permute-start.5 = (bf16[192,256]{1,0:T(8,128)(2,1)S(1)}, bf16[192,256]{1,0:T(8,128)(2,1)S(1)}, u32[]{:S(2)}, u32[]{:S(2)}) collective-permute-start(bf16[192,256]{1,0:T(8,128)(2,1)S(1)} %collective-permute-done.3), channel_id=1, source_target_pairs={{0,15},{1,0},{2,1},{3,2},{4,3},{5,4},{6,5},{7,6},{8,7},{9,8},{10,9... | collective-permute-start | bytes 294920 | tf_op jit(solution)/shard_map/ppermute | solution.py:49
  28.0 9.0 %collective-permute-start.4 = (bf16[192,256]{1,0:T(8,128)(2,1)S(1)}, bf16[192,256]{1,0:T(8,128)(2,1)S(1)}, u32[]{:S(2)}, u32[]{:S(2)}) collective-permute-start(bf16[192,256]{1,0:T(8,128)(2,1)S(1)} %collective-permute-done.2), channel_id=1, source_target_pairs={{0,1},{1,2},{2,3},{3,4},{4,5},{5,6},{6,7},{7,8},{8,9},{9,10},{10,1... | collective-permute-start | bytes 294920 | tf_op jit(solution)/shard_map/ppermute | solution.py:44
  30.9 8.1 %collective-permute-start.7 = (bf16[192,256]{1,0:T(8,128)(2,1)S(1)}, bf16[192,256]{1,0:T(8,128)(2,1)S(1)}, u32[]{:S(2)}, u32[]{:S(2)}) collective-permute-start(bf16[192,256]{1,0:T(8,128)(2,1)S(1)} %collective-permute-done.5), channel_id=1, source_target_pairs={{0,15},{1,0},{2,1},{3,2},{4,3},{5,4},{6,5},{7,6},{8,7},{9,8},{10,9... | collective-permute-start | bytes 294920 | tf_op jit(solution)/shard_map/ppermute | solution.py:49
  37.0 8.1 %collective-permute-start.6 = (bf16[192,256]{1,0:T(8,128)(2,1)S(1)}, bf16[192,256]{1,0:T(8,128)(2,1)S(1)}, u32[]{:S(2)}, u32[]{:S(2)}) collective-permute-start(bf16[192,256]{1,0:T(8,128)(2,1)S(1)} %collective-permute-done.4), channel_id=1, source_target_pairs={{0,1},{1,2},{2,3},{3,4},{4,5},{5,6},{6,7},{7,8},{8,9},{9,10},{10,1... | collective-permute-start | bytes 294920 | tf_op jit(solution)/shard_map/ppermute | solution.py:44
  39.0 8.0 %collective-permute-start.9 = (bf16[192,256]{1,0:T(8,128)(2,1)S(1)}, bf16[192,256]{1,0:T(8,128)(2,1)S(1)}, u32[]{:S(2)}, u32[]{:S(2)}) collective-permute-start(bf16[192,256]{1,0:T(8,128)(2,1)S(1)} %collective-permute-done.7), channel_id=1, source_target_pairs={{0,15},{1,0},{2,1},{3,2},{4,3},{5,4},{6,5},{7,6},{8,7},{9,8},{10,9... | collective-permute-start | bytes 294920 | tf_op jit(solution)/shard_map/ppermute | solution.py:49
  45.1 7.9 %collective-permute-start.8 = (bf16[192,256]{1,0:T(8,128)(2,1)S(1)}, bf16[192,256]{1,0:T(8,128)(2,1)S(1)}, u32[]{:S(2)}, u32[]{:S(2)}) collective-permute-start(bf16[192,256]{1,0:T(8,128)(2,1)S(1)} %collective-permute-done.6), channel_id=1, source_target_pairs={{0,1},{1,2},{2,3},{3,4},{4,5},{5,6},{6,7},{7,8},{8,9},{9,10},{10,1... | collective-permute-start | bytes 294920 | tf_op jit(solution)/shard_map/ppermute | solution.py:44
  47.0 7.9 %collective-permute-start.11 = (bf16[192,256]{1,0:T(8,128)(2,1)S(1)}, bf16[192,256]{1,0:T(8,128)(2,1)S(1)}, u32[]{:S(2)}, u32[]{:S(2)}) collective-permute-start(bf16[192,256]{1,0:T(8,128)(2,1)S(1)} %collective-permute-done.9), channel_id=1, source_target_pairs={{0,15},{1,0},{2,1},{3,2},{4,3},{5,4},{6,5},{7,6},{8,7},{9,8},{10,9... | collective-permute-start | bytes 294920 | tf_op jit(solution)/shard_map/ppermute | solution.py:49
  53.0 7.9 %collective-permute-start.10 = (bf16[192,256]{1,0:T(8,128)(2,1)S(1)}, bf16[192,256]{1,0:T(8,128)(2,1)S(1)}, u32[]{:S(2)}, u32[]{:S(2)}) collective-permute-start(bf16[192,256]{1,0:T(8,128)(2,1)S(1)} %collective-permute-done.8), channel_id=1, source_target_pairs={{0,1},{1,2},{2,3},{3,4},{4,5},{5,6},{6,7},{7,8},{8,9},{9,10},{10,1... | collective-permute-start | bytes 294920 | tf_op jit(solution)/shard_map/ppermute | solution.py:44
  55.0 7.9 %collective-permute-start.13 = (bf16[192,256]{1,0:T(8,128)(2,1)S(1)}, bf16[192,256]{1,0:T(8,128)(2,1)S(1)}, u32[]{:S(2)}, u32[]{:S(2)}) collective-permute-start(bf16[192,256]{1,0:T(8,128)(2,1)S(1)} %collective-permute-done.11), channel_id=1, source_target_pairs={{0,15},{1,0},{2,1},{3,2},{4,3},{5,4},{6,5},{7,6},{8,7},{9,8},{10,9... | collective-permute-start | bytes 294920 | tf_op jit(solution)/shard_map/ppermute | solution.py:49
  61.0 7.9 %collective-permute-start.12 = (bf16[192,256]{1,0:T(8,128)(2,1)S(1)}, bf16[192,256]{1,0:T(8,128)(2,1)S(1)}, u32[]{:S(2)}, u32[]{:S(2)}) collective-permute-start(bf16[192,256]{1,0:T(8,128)(2,1)S(1)} %collective-permute-done.10), channel_id=1, source_target_pairs={{0,1},{1,2},{2,3},{3,4},{4,5},{5,6},{6,7},{7,8},{8,9},{9,10},{10,1... | collective-permute-start | bytes 294920 | tf_op jit(solution)/shard_map/ppermute | solution.py:44
  62.9 14.0 %collective-permute-start.15 = (bf16[192,256]{1,0:T(8,128)(2,1)S(1)}, bf16[192,256]{1,0:T(8,128)(2,1)S(1)}, u32[]{:S(2)}, u32[]{:S(2)}) collective-permute-start(bf16[192,256]{1,0:T(8,128)(2,1)S(1)} %collective-permute-done.13), channel_id=1, source_target_pairs={{0,15},{1,0},{2,1},{3,2},{4,3},{5,4},{6,5},{7,6},{8,7},{9,8},{10,9... | collective-permute-start | bytes 294920 | tf_op jit(solution)/shard_map/ppermute | solution.py:49
  68.9 7.9 %collective-permute-start.14 = (bf16[192,256]{1,0:T(8,128)(2,1)S(1)}, bf16[192,256]{1,0:T(8,128)(2,1)S(1)}, u32[]{:S(2)}, u32[]{:S(2)}) collective-permute-start(bf16[192,256]{1,0:T(8,128)(2,1)S(1)} %collective-permute-done.12), channel_id=1, source_target_pairs={{0,1},{1,2},{2,3},{3,4},{4,5},{5,6},{6,7},{7,8},{8,9},{9,10},{10,1... | collective-permute-start | bytes 294920 | tf_op jit(solution)/shard_map/ppermute | solution.py:44
  76.8 7.9 %collective-permute-start.16 = (bf16[192,256]{1,0:T(8,128)(2,1)S(1)}, bf16[192,256]{1,0:T(8,128)(2,1)S(1)}, u32[]{:S(2)}, u32[]{:S(2)}) collective-permute-start(bf16[192,256]{1,0:T(8,128)(2,1)S(1)} %collective-permute-done.14), channel_id=1, source_target_pairs={{0,1},{1,2},{2,3},{3,4},{4,5},{5,6},{6,7},{7,8},{8,9},{9,10},{10,1... | collective-permute-start | bytes 294920 | tf_op jit(solution)/shard_map/ppermute | solution.py:44
Sparse Core Ops, SparseCore 0:
  118.4 71.5 reduce-scatter.1
